TPU v7x, 32 devices: a whole 2x2x4 slice. The times are simulated.
32 devices in a mesh: grp: 2 (over y), gx: 4 (over z), gy: 2 (over x), gz: 2 (over core).
Axes of the slice: x: 2, y: 2, z: 4, core: 2. Of those that a mesh axis runs over, the one named last changes fastest.
Arguments:
- parcel_values: bfloat16 [6, 131072], P(None, ('grp', 'gx', 'gy', 'gz')), parts along dimension 1, may hold values from -2304 to 2304
- parcel_owner: int32 [131072, 1], P(('grp', 'gx', 'gy', 'gz')), parts along dimension 0, may hold values from 0 to 3; in each aligned block of 4096 rows (0 to 4095, 4096 to 8191, ...) at most 1536 rows name the same one
- parcel_cell: int32 [131072], P(('grp', 'gx', 'gy', 'gz')), parts along dimension 0, may hold values from 0 to 65535
- live_counts: int32 [32], P(('grp', 'gx', 'gy', 'gz')), parts along dimension 0, may hold values from 1 to 4096, 49152 in all
- fluid_state: bfloat16 [6, 256, 32, 256], P(None, ('grp', 'gx'), 'gy', 'gz'), parts along dimension 1, may hold values from -6 to 6
Outputs:
- coupled: bfloat16 [6, 256, 32, 256], P(None, ('grp', 'gx'), 'gy', 'gz'), parts along dimension 1
There are 2 independent parts, one for each index of `grp`. A program takes and returns all parts, laid end to end along the dimension named above; each array names one. Nothing has to cross between parts.
Inputs may be any that keep to these rules, and one draw needn't show every extreme that they name: `parcel_owner`: among the rows of one brick no streamwise index is named by more than 1536 rows; some brick names one exactly 1536 times. `parcel_cell`: cells are numbered (x * 16 + y) * 128 + z within the brick. `live_counts`: A brick's live parcels are its first rows; some brick has all rows live.
All inputs are finite; a program needn't handle non-finite values. No bound on the sum of `live_counts` on one device may be relied on, other than what follows from the above.
Results may differ from a plain program's by a relative error of at most 0.005.
Values may be sent and summed in bfloat16 or wider, within the bound.
A program may use at most 64 MiB of HBM per device.

v0:
```python
import jax
import jax.numpy as jnp
from jax import lax
from jax.sharding import PartitionSpec as P

REACH = 16


spread_cells = 12.0


def padded(shard, sides, width):
    for axis, dim in sides:
        size, length = (lax.axis_size(axis), shard.shape[dim])
        up = [(i, (i + 1) % size) for i in range(size)]
        down = [(j, i) for i, j in up]
        last = lax.slice_in_dim(shard, length - width, length, axis=dim)
        initial = lax.slice_in_dim(shard, 0, width, axis=dim)
        before = lax.ppermute(last, axis, up)
        after = lax.ppermute(initial, axis, down)
        shard = jnp.concatenate([before, shard, after], axis=dim)
    return shard


def tap_curve(offsets):
    tap_grid = jnp.arange(2 * REACH + 1).astype(jnp.float32)
    tap_sum = jnp.sum(
        jnp.exp(-(tap_grid - REACH) * (tap_grid - REACH) / (2.0 * spread_cells * spread_cells))
    )
    return (
        jnp.exp(-(offsets - REACH) * (offsets - REACH) / (2.0 * spread_cells * spread_cells))
        / tap_sum
    )


def banded(out_rows, in_rows, shift):
    row_ids = lax.broadcasted_iota(jnp.int32, (out_rows, in_rows), 0)
    col_ids = lax.broadcasted_iota(jnp.int32, (out_rows, in_rows), 1)
    offset_ids = col_ids - row_ids + shift
    inside = (offset_ids >= 0) & (offset_ids <= 2 * REACH)
    values = tap_curve(offset_ids.astype(jnp.float32)).astype(jnp.bfloat16)
    return jnp.where(inside, values, jnp.zeros_like(values))


def on_device(parcel_values, parcel_owner, parcel_cell, live_counts, fluid_state):
    channels, count_dev = parcel_values.shape
    width_x, width_y, width_z = (fluid_state.shape[1], fluid_state.shape[2], fluid_state.shape[3])
    owners = lax.axis_size("gx")
    capacity = 3 * count_dev // (2 * owners)
    owner_ids = parcel_owner[:, 0]
    local_rows = jnp.arange(count_dev, dtype=jnp.int32)
    is_live = local_rows < live_counts[0]
    owner_hits = (
        (owner_ids[:, None] == jnp.arange(owners, dtype=jnp.int32)[None, :]) & is_live[:, None]
    ).astype(jnp.int32)
    position = jnp.sum(jnp.cumsum(owner_hits, axis=0) * owner_hits, axis=1) - 1
    slot_index = jnp.where(is_live, owner_ids * capacity + position, owners * capacity)
    cell_xpart = (parcel_cell // (width_y * width_z)).astype(jnp.bfloat16)
    cell_ypart = (parcel_cell // width_z % width_y).astype(jnp.bfloat16)
    cell_low = (parcel_cell % width_z).astype(jnp.bfloat16)
    send_rows = jnp.concatenate(
        [parcel_values, cell_xpart[None, :], cell_ypart[None, :], cell_low[None, :]], axis=0
    )
    packed = (
        jnp.zeros((channels + 3, owners * capacity), jnp.bfloat16)
        .at[:, slot_index]
        .set(send_rows, mode="drop")
    )
    packed = packed.reshape(channels + 3, owners, capacity)
    arrived = lax.all_to_all(packed, "gx", split_axis=1, concat_axis=1, tiled=True).reshape(
        channels + 3, owners * capacity
    )
    slot_total = owners * capacity
    block_rows = min(1024, slot_total)
    plane_cells = width_x * width_y
    high_grid = jnp.arange(plane_cells, dtype=jnp.float32)
    low_grid = jnp.arange(width_z, dtype=jnp.float32)

    def deposit(step_index, summed):
        window = lax.dynamic_slice_in_dim(arrived, step_index * block_rows, block_rows, 1)
        high_ids = window[channels].astype(jnp.float32) * width_y + window[channels + 1].astype(
            jnp.float32
        )
        high_hot = (high_ids[:, None] == high_grid[None, :]).astype(jnp.bfloat16)
        low_hot = (window[channels + 2].astype(jnp.float32)[:, None] == low_grid[None, :]).astype(
            jnp.bfloat16
        )
        weighted = window[:channels][:, :, None] * low_hot[None, :, :]
        return summed + jnp.einsum(
            "sh,csz->chz", high_hot, weighted, preferred_element_type=jnp.float32
        )

    summed = lax.fori_loop(
        0,
        slot_total // block_rows,
        deposit,
        jnp.zeros((channels, plane_cells, width_z), jnp.float32),
    )
    source = summed.reshape(channels, width_x, width_y, width_z).astype(jnp.bfloat16)
    flat_source = source.reshape(channels, width_x, width_y * width_z)
    pencil = lax.all_to_all(flat_source, "gx", split_axis=2, concat_axis=1, tiled=True)
    full_x = pencil.shape[1]
    smoothed = jnp.einsum(
        "ij,cjk->cik", banded(full_x, full_x, REACH), pencil, preferred_element_type=jnp.float32
    ).astype(jnp.bfloat16)
    after_x = lax.all_to_all(smoothed, "gx", split_axis=1, concat_axis=2, tiled=True)
    after_x = after_x.reshape(channels, width_x, width_y, width_z)
    extended_y = padded(after_x, (("gy", 2),), REACH)
    after_y = jnp.einsum(
        "ij,cxjz->cxiz",
        banded(width_y, width_y + 2 * REACH, 0),
        extended_y,
        preferred_element_type=jnp.float32,
    ).astype(jnp.bfloat16)
    extended_z = padded(after_y, (("gz", 3),), REACH)
    smooth_z = jnp.einsum(
        "cxyj,ij->cxyi",
        extended_z,
        banded(width_z, width_z + 2 * REACH, 0),
        preferred_element_type=jnp.float32,
    )
    return (fluid_state.astype(jnp.float32) + smooth_z).astype(jnp.bfloat16)


def solution(mesh):
    in_specs = (
        P(None, ("grp", "gx", "gy", "gz")),
        P(("grp", "gx", "gy", "gz"), None),
        P(("grp", "gx", "gy", "gz")),
        P(("grp", "gx", "gy", "gz")),
        P(None, ("grp", "gx"), "gy", "gz"),
    )
    out_specs = P(None, ("grp", "gx"), "gy", "gz")
    return jax.shard_map(
        on_device, mesh=mesh, in_specs=in_specs, out_specs=out_specs, check_vma=False
    )
```

profile of v0, /device:TPU:0, one launch (start us, length us, event | category | flops | bytes accessed | tf_op | source)
XLA Modules:
  0.0 157.6 jit_solution(1705467644931148753)
XLA Ops:
  0.7 0.7 fusion.61
  1.4 1.2 reduce-window.6
  3.1 0.8 fusion.53
  3.9 0.8 fusion.79
  4.8 0.9 maximum_bitcast_fusion
  6.3 11.4 %scatter_custom_fusion = bf16[9,6144]{0,1:T(8,128)(2,1)S(1)} fusion(s32[4096]{0:T(1024)S(1)} %bitcast.85, bf16[4096,9]{1,0:T(8,128)(2,1)S(1)} %copy.30, bf16[]{:T(256)} %constant.117.clone.1), kind=kCustom, calls=%fused_computation.36 | custom fusion | bytes 110594 | tf_op jit(solution)/shard_map/scatter | solution.py:67
  17.6 1.4 copy.31
  19.0 6.3 %all-to-all-start = ((bf16[9,4,1536]{2,0,1:T(8,128)(2,1)}), bf16[9,4,1536]{2,0,1:T(8,128)(2,1)S(1)}, u32[]{:S(2)}, u32[]{:S(2)}) async-start(bf16[9,4,1536]{2,0,1:T(8,128)(2,1)} %copy.31), calls=%async_computation | async-start | bytes 393216 | tf_op jit(solution)/shard_map/all_to_all | solution.py:70
  25.3 7.5 %all-to-all-done = bf16[9,4,1536]{2,0,1:T(8,128)(2,1)S(1)} async-done(((bf16[9,4,1536]{2,0,1:T(8,128)(2,1)}), bf16[9,4,1536]{2,0,1:T(8,128)(2,1)S(1)}, u32[]{:S(2)}, u32[]{:S(2)}) %all-to-all-start) | async-done | bytes 110624 | tf_op jit(solution)/shard_map/all_to_all | solution.py:70
  33.1 9.3 %while.14 = (s32[]{:T(128)}, f32[6,512,128]{1,2,0:T(8,128)S(1)}, bf16[9,6144]{1,0:T(8,128)(2,1)S(1)}, s32[]{:T(128)}, s32[]{:T(128)}, /*index=5*/s32[]{}, s32[]{:T(128)}, s32[]{:T(128)}, s32[]{}, s32[]{}) while((s32[]{:T(128)}, f32[6,512,128]{1,2,0:T(8,128)S(1)}, bf16[9,6144]{1,0:T(8,128)(2,1)S(1)}, s32[]{:T(128)}, s32[]{:T(128)}, ...), condition=%wide.region_5.6_spmd.clone, body=%wide.region_4.5_spmd.clone.sunk | while | flops 807670784 | bytes 3729625 | solution.py:93
  33.3 1.3 bitcast_add_fusion.2
  34.8 1.3 bitcast_add_fusion.2
  36.4 1.3 bitcast_add_fusion.2
  37.9 1.3 bitcast_add_fusion.2
  39.5 1.3 bitcast_add_fusion.2
  41.0 1.3 bitcast_add_fusion.2
  43.2 4.2 %copy.34 = bf16[6,32,2048]{1,0,2:T(8,128)(2,1)} copy(bf16[6,32,2048]{2,1,0:T(8,128)(2,1)S(1)} %convert_element_type.120) | data formatting | bytes 1572864 | tf_op jit(solution)/shard_map/convert_element_type | solution.py:99
  47.4 5.7 %reshape.138 = bf16[4,2,49152]{2,1,0:T(2,128)(2,1)} reshape(bf16[2048,6,32]{2,1,0:T(8,128)(2,1)} %bitcast.72) | data formatting | bytes 1572864
  53.1 3.5 %all-to-all-start.1 = ((bf16[4,2,49152]{2,1,0:T(2,128)(2,1)}), bf16[4,2,49152]{2,1,0:T(2,128)(2,1)S(1)}, u32[]{:S(2)}, u32[]{:S(2)}) async-start(bf16[4,2,49152]{2,1,0:T(2,128)(2,1)} %reshape.138), calls=%async_computation.1 | async-start | bytes 1572864 | tf_op jit(solution)/shard_map/all_to_all | solution.py:101
  57.2 18.1 %all-to-all-done.1 = bf16[4,2,49152]{2,1,0:T(2,128)(2,1)S(1)} async-done(((bf16[4,2,49152]{2,1,0:T(2,128)(2,1)}), bf16[4,2,49152]{2,1,0:T(2,128)(2,1)S(1)}, u32[]{:S(2)}, u32[]{:S(2)}) %all-to-all-start.1) | async-done | bytes 786464 | tf_op jit(solution)/shard_map/all_to_all | solution.py:101
  75.3 4.2 %reshape.139 = bf16[2048,6,32]{2,1,0:T(8,128)(2,1)} reshape(bf16[4,2,49152]{2,1,0:T(2,128)(2,1)S(1)} %all-to-all-done.1) | data formatting | bytes 1572864
  79.5 4.5 %copy.48 = bf16[6,32,4,512]{3,2,1,0:T(4,128)(2,1)S(1)} copy(bf16[6,32,4,512]{1,0,3,2:T(8,128)(2,1)} %bitcast.73) | data formatting | bytes 1572864 | tf_op jit(solution)/shard_map/all_to_all | solution.py:101
  84.2 1.0 fusion.38
  85.2 0.9 copy.38
  86.1 27.7 %all_to_all.38 = bf16[6,128,512]{2,0,1:T(8,128)(2,1)S(1)} all-to-all(bf16[6,128,512]{2,0,1:T(8,128)(2,1)S(1)} %copy.38), channel_id=1, replica_groups=mesh['grp'=2,'gx'=4,'gy'=2,'gz'=2] {'gx'}, dimensions={1} | all-to-all | bytes 1572864 | tf_op jit(solution)/shard_map/all_to_all | solution.py:106
  114.7 1.6 collective-permute-start
  116.8 18.5 %collective-permute-done = bf16[6,32,16,128]{3,2,1,0:T(8,128)(2,1)S(1)} collective-permute-done((bf16[6,32,16,128]{3,2,1,0:T(8,128)(2,1)S(1)}, bf16[6,32,16,128]{3,2,1,0:T(8,128)(2,1)S(1)}, u32[]{:S(2)}, u32[]{:S(2)}) %collective-permute-start) | collective-permute-done | bytes 786464 | tf_op jit(solution)/shard_map/ppermute | solution.py:19
  135.2 14.4 %collective-permute-done.1 = bf16[6,32,16,128]{3,2,1,0:T(8,128)(2,1)S(1)} collective-permute-done((bf16[6,32,16,128]{3,2,1,0:T(8,128)(2,1)S(1)}, bf16[6,32,16,128]{3,2,1,0:T(8,128)(2,1)S(1)}, u32[]{:S(2)}, u32[]{:S(2)}) %collective-permute-start.1) | collective-permute-done | bytes 786464 | tf_op jit(solution)/shard_map/ppermute | solution.py:20
  149.7 1.1 fusion.35
  153.5 0.6 copy.43
  154.3 0.6 copy.44
  155.0 2.6 %add_convert_fusion = bf16[6,32,16,128]{3,2,1,0:T(8,128)(2,1)} fusion(bf16[6,32,16,128]{3,2,1,0:T(8,128)(2,1)S(1)} %copy-done.1, bf16[6,32,16,16]{3,2,1,0:T(8,128)(2,1)S(1)} %copy.44, bf16[6,32,16,128]{3,2,1,0:T(8,128)(2,1)S(1)} %fusion.35, bf16[6,32,16,16]{3,2,1,0:T(8,128)(2,1)S(1)} %copy.43, f32[]{:T(128)} %fusion.104), kind=kOutput, calls=%fused_computation.31 | convolution fusion | flops 130203648 | bytes 2555908 | tf_op jit(solution)/shard_map/cxyj,ij->cxyi/dot_general | solution.py:116
  (58 shorter events, 8.4 us)
Async XLA Ops:
  0.0 6.2 %copy-start = (s32[4096,1]{0,1:T(1,128)S(1)}, s32[4096,1]{0,1:T(1,128)}, u32[]{:S(2)}) copy-start(s32[4096,1]{0,1:T(1,128)} %param.8) | copy-start | bytes 49156
  19.0 13.8 %all-to-all-start = ((bf16[9,4,1536]{2,0,1:T(8,128)(2,1)}), bf16[9,4,1536]{2,0,1:T(8,128)(2,1)S(1)}, u32[]{:S(2)}, u32[]{:S(2)}) async-start(bf16[9,4,1536]{2,0,1:T(8,128)(2,1)} %copy.31), calls=%async_computation | async-start | bytes 393216 | tf_op jit(solution)/shard_map/all_to_all | solution.py:70
  53.1 22.2 %all-to-all-start.1 = ((bf16[4,2,49152]{2,1,0:T(2,128)(2,1)}), bf16[4,2,49152]{2,1,0:T(2,128)(2,1)S(1)}, u32[]{:S(2)}, u32[]{:S(2)}) async-start(bf16[4,2,49152]{2,1,0:T(2,128)(2,1)} %reshape.138), calls=%async_computation.1 | async-start | bytes 1572864 | tf_op jit(solution)/shard_map/all_to_all | solution.py:101
  114.7 20.5 %collective-permute-start = (bf16[6,32,16,128]{3,2,1,0:T(8,128)(2,1)S(1)}, bf16[6,32,16,128]{3,2,1,0:T(8,128)(2,1)S(1)}, u32[]{:S(2)}, u32[]{:S(2)}) collective-permute-start(bf16[6,32,16,128]{3,2,1,0:T(8,128)(2,1)S(1)} %reshape.120), channel_id=1, source_target_pairs={{0,2},{2,0},{1,3},{3,1},{4,6},{6,4},{5,7},{7,5},{8,10},{10,8},{9,1... | collective-permute-start | bytes 2359304 | tf_op jit(solution)/shard_map/ppermute | solution.py:19
  116.2 33.4 %collective-permute-start.1 = (bf16[6,32,16,128]{3,2,1,0:T(8,128)(2,1)S(1)}, bf16[6,32,16,128]{3,2,1,0:T(8,128)(2,1)S(1)}, u32[]{:S(2)}, u32[]{:S(2)}) collective-permute-start(bf16[6,32,16,128]{3,2,1,0:T(8,128)(2,1)S(1)} %reshape.120), channel_id=1, source_target_pairs={{2,0},{0,2},{3,1},{1,3},{6,4},{4,6},{7,5},{5,7},{10,8},{8,10},{11,... | collective-permute-start | bytes 2359304 | tf_op jit(solution)/shard_map/ppermute | solution.py:20
  151.7 1.8 %collective-permute-start.2 = (bf16[6,32,16,16]{1,3,2,0:T(8,128)(2,1)S(1)}, bf16[6,32,16,16]{1,3,2,0:T(8,128)(2,1)S(1)}, u32[]{:S(2)}, u32[]{:S(2)}) collective-permute-start(bf16[6,32,16,16]{1,3,2,0:T(8,128)(2,1)S(1)} %copy.41), channel_id=1, source_target_pairs={{0,1},{1,0},{2,3},{3,2},{4,5},{5,4},{6,7},{7,6},{8,9},{9,8},{10,11... | collective-permute-start | bytes 294920 | tf_op jit(solution)/shard_map/ppermute | solution.py:19
  151.8 3.2 %copy-start.1 = (bf16[6,32,16,128]{3,2,1,0:T(8,128)(2,1)S(1)}, bf16[6,32,16,128]{3,2,1,0:T(8,128)(2,1)}, u32[]{:S(2)}) copy-start(bf16[6,32,16,128]{3,2,1,0:T(8,128)(2,1)} %param.11) | copy-start | bytes 2359300
  152.5 1.9 %collective-permute-start.3 = (bf16[6,32,16,16]{1,3,2,0:T(8,128)(2,1)S(1)}, bf16[6,32,16,16]{1,3,2,0:T(8,128)(2,1)S(1)}, u32[]{:S(2)}, u32[]{:S(2)}) collective-permute-start(bf16[6,32,16,16]{1,3,2,0:T(8,128)(2,1)S(1)} %copy.42), channel_id=1, source_target_pairs={{1,0},{0,1},{3,2},{2,3},{5,4},{4,5},{7,6},{6,7},{9,8},{8,9},{11,10... | collective-permute-start | bytes 294920 | tf_op jit(solution)/shard_map/ppermute | solution.py:20
where the time goes:
time: 158 us
  waiting for transfers between devices  59.2 us (37%)
  local copies, waits for them, and re-layouts  37.9 us (24%)
  blocking collectives  27.7 us (18%)
  matrix products  12.6 us (8%)
  starting transfers between devices  12.5 us (8%)
  other arithmetic  6.49 us (4%)
    all_to_all x1, blocking collectives, on_device(): lax.all_to_all(smoothed, 'gx', split_axis=1, concat_axis=2, tiled=True)  27.7 us
    ppermute x2, waiting for transfers between devices, padded(): before = lax.ppermute(last, axis, up)  19 us
    all_to_all x1, waiting for transfers between devices, on_device(): lax.all_to_all(flat_source, 'gx', split_axis=2, concat_axis=1, tiled=True)  18.1 us
    ppermute x2, waiting for transfers between devices, padded(): after = lax.ppermute(initial, axis, down)  14.6 us
    scatter x1, local copies, waits for them, and re-layouts, on_device(): packed = jnp.zeros((channels + 3, owners * capacity), jnp.bfloat16).at[:,...  11.4 us
    unnamed x8, local copies, waits for them, and re-layouts  9.98 us
    dot_general x6, matrix products, deposit(): jnp.einsum('sh,csz->chz', high_hot, weighted, preferred_element_type=jnp....  7.91 us
    all_to_all x1, waiting for transfers between devices, on_device(): lax.all_to_all(packed, 'gx', split_axis=1, concat_axis=1, tiled=True)  7.51 us
  transfers between devices with their start and end apart: 6, of which 6 were waited for; matrix products, arithmetic and copies ran while one was open for 1% of the time, Pallas kernels for 0%

commit v1 on v0

--- a/solution.py
+++ b/solution.py
@@ -1,6 +1,12 @@
+import functools
+import math
+
 import jax
 import jax.numpy as jnp
+import numpy as np
 from jax import lax
+from jax.experimental import pallas as pl
+from jax.experimental.pallas import tpu as pltpu
 from jax.sharding import PartitionSpec as P
 
 REACH = 16
@@ -42,7 +48,15 @@
     return jnp.where(inside, values, jnp.zeros_like(values))
 
 
-def on_device(parcel_values, parcel_owner, parcel_cell, live_counts, fluid_state):
+def running_sum(hits):
+    shift = 1
+    while shift < hits.shape[0]:
+        hits = hits + jnp.pad(hits[:-shift], ((shift, 0), (0, 0)))
+        shift *= 2
+    return hits
+
+
+def general(parcel_values, parcel_owner, parcel_cell, live_counts, fluid_state):
     channels, count_dev = parcel_values.shape
     width_x, width_y, width_z = (fluid_state.shape[1], fluid_state.shape[2], fluid_state.shape[3])
     owners = lax.axis_size("gx")
@@ -53,7 +67,7 @@
     owner_hits = (
         (owner_ids[:, None] == jnp.arange(owners, dtype=jnp.int32)[None, :]) & is_live[:, None]
     ).astype(jnp.int32)
-    position = jnp.sum(jnp.cumsum(owner_hits, axis=0) * owner_hits, axis=1) - 1
+    position = jnp.sum(running_sum(owner_hits) * owner_hits, axis=1) - 1
     slot_index = jnp.where(is_live, owner_ids * capacity + position, owners * capacity)
     cell_xpart = (parcel_cell // (width_y * width_z)).astype(jnp.bfloat16)
     cell_ypart = (parcel_cell // width_z % width_y).astype(jnp.bfloat16)
@@ -122,7 +136,196 @@
     return (fluid_state.astype(jnp.float32) + smooth_z).astype(jnp.bfloat16)
 
 
+SEG = 256
+STEP = 4
+FIELDS = 3
+PAIR = 2
+FAR = 1024.0
+TAP_SUM = float(
+    sum(math.exp(-((t - REACH) ** 2) / (2.0 * spread_cells**2)) for t in range(2 * REACH + 1))
+)
+
+
+def tap_matrix(offsets):
+    values = np.exp(-((offsets - REACH) ** 2) / (2.0 * spread_cells**2)) / TAP_SUM
+    values = values.astype(np.float32).astype(jnp.bfloat16).astype(np.float32)
+    return np.where((offsets >= 0) & (offsets <= 2 * REACH), values, 0.0)
+
+
+def periodic_pair(width):
+    out_at, in_at = np.arange(width)[:, None], np.arange(width)[None, :]
+    own = tap_matrix(in_at - out_at + REACH)
+    other = tap_matrix(in_at - width - out_at + REACH) + tap_matrix(in_at + width - out_at + REACH)
+    return own, other
+
+
+def fused(sizes, pay_ref, fluid_ref, wy_ref, wz_ref, out_ref, arrived, fields, weights, total,
+          x_buf, x_in, z_buf, z_in, pay_send, pay_recv, zs_send, zs_recv, ys_send, ys_recv):
+    owners, channels, width_x, width_y, width_z = sizes
+    plane, lanes = width_x * width_y, SEG * STEP
+    rows = pay_ref.shape[0]
+    steps = rows // STEP
+    groups = channels // PAIR
+    gx, gy, gz = lax.axis_index("gx"), lax.axis_index("gy"), lax.axis_index("gz")
+    mesh_id = pl.DeviceIdType.MESH
+
+    barrier = pltpu.get_barrier_semaphore()
+    for hop in range(1, owners):
+        pl.semaphore_signal(barrier, inc=1, device_id={"gx": (gx + hop) % owners}, device_id_type=mesh_id)
+    pl.semaphore_signal(barrier, inc=1, device_id={"gy": 1 - gy}, device_id_type=mesh_id)
+    pl.semaphore_signal(barrier, inc=1, device_id={"gz": 1 - gz}, device_id_type=mesh_id)
+    pl.semaphore_wait(barrier, owners + 1)
+
+    sends = []
+    for hop in range(1, owners):
+        copy = pltpu.make_async_remote_copy(
+            src_ref=pay_ref, dst_ref=arrived.at[hop - 1], send_sem=pay_send.at[hop - 1],
+            recv_sem=pay_recv.at[hop - 1], device_id={"gx": (gx + hop) % owners}, device_id_type=mesh_id)
+        copy.start()
+        sends.append(copy)
+
+    z_ids = lax.broadcasted_iota(jnp.int32, (width_z, lanes), 0).astype(jnp.float32)
+    x_ids = (lax.broadcasted_iota(jnp.int32, (width_x, lanes), 0) + gx * width_x).astype(jnp.float32)
+    y_ids = lax.broadcasted_iota(jnp.int32, (width_y, lanes), 0).astype(jnp.float32)
+
+    def field(slot, step, which):
+        return jnp.concatenate(
+            [fields[slot, pl.ds(step * STEP + j, 1), which * SEG:(which + 1) * SEG] for j in range(STEP)],
+            axis=1)
+
+    def build(slot, step):
+        away = field(slot, step, channels) - x_ids
+        taps = jnp.exp(-(away * away) / (2.0 * spread_cells * spread_cells)) / TAP_SUM
+        taps = jnp.where(jnp.abs(away) <= REACH, taps, 0.0).astype(jnp.bfloat16).astype(jnp.float32)
+        hit = jnp.where(field(slot, step, channels + 1) == y_ids, 1.0, 0.0)
+        for x in range(width_x):
+            weights[slot * steps + step, x * width_y:(x + 1) * width_y, :] = (
+                taps[x:x + 1, :] * hit).astype(jnp.bfloat16)
+
+    def add(slot, step, group):
+        here = field(slot, step, channels + 2) == z_ids
+        spread = jnp.concatenate(
+            [jnp.where(here, field(slot, step, group * PAIR + k), 0.0).astype(jnp.bfloat16)
+             for k in range(PAIR)], axis=0)
+        total[...] += lax.dot_general(
+            weights[slot * steps + step], spread, (((1,), (1,)), ((), ())),
+            preferred_element_type=jnp.float32)
+
+    def deposit(first, last, group, building):
+        def body(i, carry):
+            slot, step = i // steps, i % steps
+            if building:
+                build(slot, step)
+            add(slot, step, group)
+            return carry
+
+        lax.fori_loop(first * steps, last * steps, body, 0)
+
+    def swap_z(group):
+        x_buf[group] = total[...].astype(jnp.bfloat16)
+        copy = pltpu.make_async_remote_copy(
+            src_ref=x_buf.at[group], dst_ref=x_in.at[group], send_sem=zs_send.at[group],
+            recv_sem=zs_recv.at[group], device_id={"gz": 1 - gz}, device_id_type=mesh_id)
+        copy.start()
+        return copy
+
+    def filter_z(group, copy):
+        copy.wait_recv()
+        for k in range(PAIR):
+            at = slice(k * width_z, (k + 1) * width_z)
+            both = jnp.concatenate([x_buf[group, :, at], x_in[group, :, at]], axis=1)
+            z_buf[group, :, at] = jnp.dot(
+                both, wz_ref[...], preferred_element_type=jnp.float32).astype(jnp.bfloat16)
+        sent = pltpu.make_async_remote_copy(
+            src_ref=z_buf.at[group], dst_ref=z_in.at[group], send_sem=ys_send.at[group],
+            recv_sem=ys_recv.at[group], device_id={"gy": 1 - gy}, device_id_type=mesh_id)
+        sent.start()
+        return sent
+
+    block = wy_ref.shape[0]
+
+    def filter_y(group, copy):
+        copy.wait_recv()
+        for b in range(plane // block):
+            at = slice(b * block, (b + 1) * block)
+            both = jnp.concatenate([z_buf[group, at, :], z_in[group, at, :]], axis=0)
+            smooth = jnp.dot(wy_ref[...], both, preferred_element_type=jnp.float32)
+            for k in range(PAIR):
+                out_ref[group * PAIR + k, at, :] = (
+                    fluid_ref[group * PAIR + k, at, :].astype(jnp.float32)
+                    + smooth[:, k * width_z:(k + 1) * width_z]).astype(jnp.bfloat16)
+
+    fields[0] = pay_ref[...].astype(jnp.float32)
+    total[...] = jnp.zeros_like(total)
+    for slot in range(owners):
+        if slot:
+            sends[slot - 1].wait_recv()
+            fields[slot] = arrived[slot - 1].astype(jnp.float32)
+        deposit(slot, slot + 1, 0, True)
+    z_copies, y_copies = [swap_z(0)], []
+    for group in range(1, groups):
+        total[...] = jnp.zeros_like(total)
+        deposit(0, 1, group, False)
+        y_copies.append(filter_z(group - 1, z_copies[-1]))
+        deposit(1, owners, group, False)
+        z_copies.append(swap_z(group))
+    y_copies.append(filter_z(groups - 1, z_copies[-1]))
+    for group in range(groups):
+        filter_y(group, y_copies[group])
+    for copy in (*sends, *z_copies, *y_copies):
+        copy.wait_send()
+
+
+def on_device(parcel_values, parcel_owner, parcel_cell, live_counts, fluid_state):
+    channels, count_dev = parcel_values.shape
+    width_x, width_y, width_z = fluid_state.shape[1:]
+    owners, plane, rows = lax.axis_size("gx"), width_x * width_y, count_dev // SEG
+    is_live = jnp.arange(count_dev, dtype=jnp.int32) < live_counts[0]
+    cell_x = jnp.where(is_live, parcel_owner[:, 0] * width_x + parcel_cell // (width_y * width_z), int(FAR))
+    cell_y, cell_z = parcel_cell // width_z % width_y, parcel_cell % width_z
+    payload = jnp.concatenate(
+        [parcel_values[k].reshape(rows, SEG) for k in range(channels)]
+        + [c.astype(jnp.bfloat16).reshape(rows, SEG) for c in (cell_x, cell_y, cell_z)], axis=1)
+    own_y, other_y = periodic_pair(width_y)
+    repeat = np.eye(256 // width_y, dtype=np.float32)
+    weight_y = np.concatenate([np.kron(repeat, own_y), np.kron(repeat, other_y)], axis=1)
+    own_z, other_z = periodic_pair(width_z)
+    weight_z = np.concatenate([own_z.T, other_z.T], axis=0)
+    sizes = (owners, channels, width_x, width_y, width_z)
+    groups, wide = channels // PAIR, PAIR * width_z
+    vmem = pl.BlockSpec(memory_space=pltpu.VMEM)
+    coupled = pl.pallas_call(
+        functools.partial(fused, sizes),
+        out_shape=jax.ShapeDtypeStruct((channels, plane, width_z), jnp.bfloat16),
+        in_specs=[vmem] * 4,
+        out_specs=vmem,
+        scratch_shapes=[
+            pltpu.VMEM((owners - 1, rows, (channels + FIELDS) * SEG), jnp.bfloat16),
+            pltpu.VMEM((owners, rows, (channels + FIELDS) * SEG), jnp.float32),
+            pltpu.VMEM((owners * (rows // STEP), plane, SEG * STEP), jnp.bfloat16),
+            pltpu.VMEM((plane, wide), jnp.float32),
+            pltpu.VMEM((groups, plane, wide), jnp.bfloat16),
+            pltpu.VMEM((groups, plane, wide), jnp.bfloat16),
+            pltpu.VMEM((groups, plane, wide), jnp.bfloat16),
+            pltpu.VMEM((groups, plane, wide), jnp.bfloat16),
+            pltpu.SemaphoreType.DMA((owners - 1,)),
+            pltpu.SemaphoreType.DMA((owners - 1,)),
+            pltpu.SemaphoreType.DMA((groups,)),
+            pltpu.SemaphoreType.DMA((groups,)),
+            pltpu.SemaphoreType.DMA((groups,)),
+            pltpu.SemaphoreType.DMA((groups,)),
+        ],
+        compiler_params=pltpu.CompilerParams(
+            collective_id=0, has_side_effects=True, vmem_limit_bytes=48 << 20
+        ),
+    )(payload, fluid_state.reshape(channels, plane, width_z),
+      jnp.asarray(weight_y, jnp.bfloat16), jnp.asarray(weight_z, jnp.bfloat16))
+    return coupled.reshape(fluid_state.shape)
+
+
 def solution(mesh):
+    small = mesh.shape["gy"] == 2 and mesh.shape["gz"] == 2 and 2 <= mesh.shape["gx"] <= 4
+    body = on_device if small else general
     in_specs = (
         P(None, ("grp", "gx", "gy", "gz")),
         P(("grp", "gx", "gy", "gz"), None),
@@ -132,5 +335,5 @@
     )
     out_specs = P(None, ("grp", "gx"), "gy", "gz")
     return jax.shard_map(
-        on_device, mesh=mesh, in_specs=in_specs, out_specs=out_specs, check_vma=False
-    )
+        body, mesh=mesh, in_specs=in_specs, out_specs=out_specs, check_vma=False
+    )

time: 158 us -> 46.5 us (0.29)
  waiting for transfers between devices: 59.2 us -> 0 us
  Pallas kernels: 0 us -> 41.4 us
  local copies, waits for them, and re-layouts: 37.9 us -> 3.17 us
  blocking collectives: 27.7 us -> 0 us
  matrix products: 12.6 us -> 0 us
  starting transfers between devices: 12.5 us -> 0 us
  other arithmetic: 6.49 us -> 0.8 us
    pallas_call x0 -> x1, Pallas kernels: none -> 41.4 us  [on_device(): pl.pallas_call(functools.partial(fused, sizes), out_shape=jax.ShapeDtypeS...]
    ppermute x4 -> x0, waiting for transfers between devices: 33.6 us -> none  [the longest x2 19 us: padded(): before = lax.ppermute(last, axis, up)]
    all_to_all x1 -> x0, blocking collectives: 27.7 us -> none  [on_device(): lax.all_to_all(smoothed, 'gx', split_axis=1, concat_axis=2, tiled=True)]
    all_to_all x2 -> x0, waiting for transfers between devices: 25.6 us -> none  [the longest x1 18.1 us: on_device(): lax.all_to_all(flat_source, 'gx', split_axis=2, concat_axis=1, tiled=True)]
    dot_general x9 -> x0, matrix products: 12.6 us -> none  [the longest x6 7.91 us: deposit(): jnp.einsum('sh,csz->chz', high_hot, weighted, preferred_element_type=jnp....]
    scatter x1 -> x0, local copies, waits for them, and re-layouts: 11.4 us -> none  [on_device(): packed = jnp.zeros((channels + 3, owners * capacity), jnp.bfloat16).at[:,...]
    all_to_all x2 -> x0, starting transfers between devices: 9.81 us -> none  [the longest x1 6.32 us: on_device(): lax.all_to_all(packed, 'gx', split_axis=1, concat_axis=1, tiled=True)]
    unnamed x8 -> x19, local copies, waits for them, and re-layouts: 9.98 us -> 2.82 us
  transfers between devices with their start and end apart: 6 -> 0, of which waited for: 6 -> 0; matrix products, arithmetic and copies ran while one was open for 1% -> 0% of each run, Pallas kernels for 0% -> 0%
where the time goes in v1:
time: 46.5 us; the launch traced here: 46.2 us
  Pallas kernels  41.4 us (89%)
  local copies, waits for them, and re-layouts  3.17 us (7%)
  between operations  0.85 us (2%)
  other arithmetic  0.8 us (2%)
    pallas_call x1, Pallas kernels, on_device(): pl.pallas_call(functools.partial(fused, sizes), out_shape=jax.ShapeDtypeS...  41.4 us
    unnamed x19, local copies, waits for them, and re-layouts  2.82 us

profile of v1, /device:TPU:0, one launch (start us, length us, event | category | flops | bytes accessed | tf_op | source)
XLA Modules:
  0.0 46.2 jit_solution(16137360569124838588)
XLA Ops:
  0.7 0.0 copy-start.4
  0.7 0.0 copy-start.3
  0.7 0.8 %broadcast_multiply_fusion = s32[4096,1]{0,1:T(1,128)S(1)} fusion(s32[4096,1]{0,1:T(1,128)} %param.8), kind=kLoop, calls=%fused_computation.37 | loop fusion | flops 4096 | bytes 32768 | tf_op jit(solution)/shard_map/mul | solution.py:284
  1.4 0.0 copy-start.1
  1.5 0.0 copy-done.4
  1.6 0.0 copy-done.3
  1.6 0.3 slice_reduce_fusion
  1.9 0.0 copy-start.2
  2.0 0.4 copy-done.1
  2.4 0.4 copy-done.2
  2.8 0.0 copy-start
  2.8 1.1 %copy-done = bf16[6,32,16,128]{3,2,1,0:T(8,128)(2,1)S(1)} copy-done((bf16[6,32,16,128]{3,2,1,0:T(8,128)(2,1)S(1)}, bf16[6,32,16,128]{3,2,1,0:T(8,128)(2,1)}, u32[]{:S(2)}) %copy-start) | copy-done | bytes 786456
  3.9 41.4 %shard_map.73 = bf16[6,512,128]{2,1,0:T(8,128)(2,1)S(1)} custom-call(bf16[16,2304]{1,0:T(8,128)(2,1)S(1)} %constant_dynamic-update-slice_fusion.pay_ref, bf16[6,512,128]{2,1,0:T(8,128)(2,1)S(1)} %bitcast.6, bf16[256,512]{1,0:T(8,128)(2,1)S(1)} %copy-done.1, bf16[256,128]{1,0:T(8,128)(2,1)S(1)} %copy-done.2), custom_call_target="tpu_custom_call" | custom-call | tf_op jit(solution)/shard_map/pallas_call | solution.py:297
  45.3 0.9 %copy.18 = bf16[6,32,16,128]{3,2,1,0:T(8,128)(2,1)} copy(bf16[6,32,16,128]{3,2,1,0:T(8,128)(2,1)S(1)} %bitcast.5) | data formatting | bytes 1572864
  (19 shorter events, 0.2 us)
Async XLA Ops:
  0.7 0.8 %copy-start.4 = (s32[4096]{0:T(1024)S(1)}, s32[4096]{0:T(1024)}, u32[]{:S(2)}) copy-start(s32[4096]{0:T(1024)} %param.9) | copy-start | bytes 49156
  0.7 0.9 %copy-start.3 = (bf16[6,4096]{1,0:T(8,128)(2,1)S(1)}, bf16[6,4096]{1,0:T(8,128)(2,1)}, u32[]{:S(2)}) copy-start(bf16[6,4096]{1,0:T(8,128)(2,1)} %param.7) | copy-start | bytes 147460
  1.4 1.0 %copy-start.1 = (bf16[256,512]{1,0:T(8,128)(2,1)S(1)}, bf16[256,512]{1,0:T(8,128)(2,1)}, u32[]{:S(2)}) copy-start(bf16[256,512]{1,0:T(8,128)(2,1)} %constant.58.clone.wy_ref) | copy-start | bytes 786436
  1.9 0.9 %copy-start.2 = (bf16[256,128]{1,0:T(8,128)(2,1)S(1)}, bf16[256,128]{1,0:T(8,128)(2,1)}, u32[]{:S(2)}) copy-start(bf16[256,128]{1,0:T(8,128)(2,1)} %constant.59.clone.wz_ref) | copy-start | bytes 196612
  2.8 1.1 %copy-start = (bf16[6,32,16,128]{3,2,1,0:T(8,128)(2,1)S(1)}, bf16[6,32,16,128]{3,2,1,0:T(8,128)(2,1)}, u32[]{:S(2)}) copy-start(bf16[6,32,16,128]{3,2,1,0:T(8,128)(2,1)} %param.11) | copy-start | bytes 2359300

commit v2 on v1

--- a/solution.py
+++ b/solution.py
@@ -159,27 +159,62 @@
     return own, other
 
 
-def fused(sizes, pay_ref, fluid_ref, wy_ref, wz_ref, out_ref, arrived, fields, weights, total,
-          x_buf, x_in, z_buf, z_in, pay_send, pay_recv, zs_send, zs_recv, ys_send, ys_recv):
+def log2(size):
+    return size.bit_length() - 1
+
+
+def fused(sizes, values_hbm, owner_hbm, cell_hbm, live_ref, fluid_hbm, wy_hbm, wz_hbm, out_ref,
+          values_ref, owner_ref, cell_ref, payload, arrived, fields, plain, weights, total, fluid, wy, wz, one, one_in, two, two_in,
+          load_sem, pay_send, pay_recv, one_send, one_recv, two_send, two_recv):
     owners, channels, width_x, width_y, width_z = sizes
     plane, lanes = width_x * width_y, SEG * STEP
-    rows = pay_ref.shape[0]
+    rows = payload.shape[0]
     steps = rows // STEP
     groups = channels // PAIR
     gx, gy, gz = lax.axis_index("gx"), lax.axis_index("gy"), lax.axis_index("gz")
     mesh_id = pl.DeviceIdType.MESH
+
+    loads = []
+    pairs = ((values_hbm, values_ref), (owner_hbm, owner_ref), (cell_hbm, cell_ref),
+             (fluid_hbm, fluid), (wy_hbm, wy), (wz_hbm, wz))
+    for at, (source, dest) in enumerate(pairs):
+        copy = pltpu.make_async_copy(source, dest, load_sem.at[at])
+        copy.start()
+        loads.append(copy)
 
     barrier = pltpu.get_barrier_semaphore()
     for hop in range(1, owners):
         pl.semaphore_signal(barrier, inc=1, device_id={"gx": (gx + hop) % owners}, device_id_type=mesh_id)
     pl.semaphore_signal(barrier, inc=1, device_id={"gy": 1 - gy}, device_id_type=mesh_id)
     pl.semaphore_signal(barrier, inc=1, device_id={"gz": 1 - gz}, device_id_type=mesh_id)
+
+    for copy in loads[:3]:
+        copy.wait()
+    width = cell_ref.shape[1]
+    row_ids = lax.broadcasted_iota(jnp.int32, cell_ref.shape, 0) * width
+    is_live = row_ids + lax.broadcasted_iota(jnp.int32, cell_ref.shape, 1) < live_ref[0]
+    cell = cell_ref[...]
+    cell_x = owner_ref[...] * width_x + lax.shift_right_logical(cell, log2(width_y * width_z))
+    cells = (
+        jnp.where(is_live, cell_x.astype(jnp.float32), FAR),
+        (lax.shift_right_logical(cell, log2(width_z)) & (width_y - 1)).astype(jnp.float32),
+        (cell & (width_z - 1)).astype(jnp.float32),
+    )
+    plain[...] = values_ref[...].astype(jnp.float32)
+    for row in range(rows):
+        for k in range(channels):
+            fields[0, row:row + 1, k * SEG:(k + 1) * SEG] = plain[k:k + 1, row * SEG:(row + 1) * SEG]
+        for k, part in enumerate(cells):
+            for j in range(SEG // width):
+                start, line = (channels + k) * SEG + j * width, row * (SEG // width) + j
+                fields[0, row:row + 1, start:start + width] = part[line:line + 1, :]
+    payload[...] = fields[0].astype(jnp.bfloat16)
     pl.semaphore_wait(barrier, owners + 1)
 
     sends = []
     for hop in range(1, owners):
         copy = pltpu.make_async_remote_copy(
-            src_ref=pay_ref, dst_ref=arrived.at[hop - 1], send_sem=pay_send.at[hop - 1],
+            src_ref=payload, dst_ref=arrived.at[hop - 1], send_sem=pay_send.at[hop - 1],
             recv_sem=pay_recv.at[hop - 1], device_id={"gx": (gx + hop) % owners}, device_id_type=mesh_id)
         copy.start()
         sends.append(copy)
@@ -207,7 +242,7 @@
         spread = jnp.concatenate(
             [jnp.where(here, field(slot, step, group * PAIR + k), 0.0).astype(jnp.bfloat16)
              for k in range(PAIR)], axis=0)
-        total[...] += lax.dot_general(
+        total[group] += lax.dot_general(
             weights[slot * steps + step], spread, (((1,), (1,)), ((), ())),
             preferred_element_type=jnp.float32)
 
@@ -219,60 +254,82 @@
             add(slot, step, group)
             return carry
 
-        lax.fori_loop(first * steps, last * steps, body, 0)
-
-    def swap_z(group):
-        x_buf[group] = total[...].astype(jnp.bfloat16)
+        lax.fori_loop(first * steps, last * steps, body, 0, unroll=steps)
+
+    def swap(group, axis, buffer, landing, sent, received):
+        me = gy if axis == "gy" else gz
         copy = pltpu.make_async_remote_copy(
-            src_ref=x_buf.at[group], dst_ref=x_in.at[group], send_sem=zs_send.at[group],
-            recv_sem=zs_recv.at[group], device_id={"gz": 1 - gz}, device_id_type=mesh_id)
+            src_ref=buffer.at[group], dst_ref=landing.at[group], send_sem=sent.at[group],
+            recv_sem=received.at[group], device_id={axis: 1 - me}, device_id_type=mesh_id)
         copy.start()
         return copy
 
-    def filter_z(group, copy):
+    def begin(group, axis):
+        one[group] = total[group].astype(jnp.bfloat16)
+        return swap(group, axis, one, one_in, one_send, one_recv)
+
+    block = wy_hbm.shape[0]
+    column = [slice(k * width_z, (k + 1) * width_z) for k in range(PAIR)]
+    spans = [slice(b * block, (b + 1) * block) for b in range(plane // block)]
+
+    def along_z(own, other, group, k):
+        both = jnp.concatenate([own[group, :, column[k]], other[group, :, column[k]]], axis=1)
+        return jnp.dot(both, wz[...], preferred_element_type=jnp.float32)
+
+    def along_y(own, other, group, span):
+        both = jnp.concatenate([own[group, span, :], other[group, span, :]], axis=0)
+        return jnp.dot(wy[...], both, preferred_element_type=jnp.float32)
+
+    def z_then_send_y(group, copy):
         copy.wait_recv()
         for k in range(PAIR):
-            at = slice(k * width_z, (k + 1) * width_z)
-            both = jnp.concatenate([x_buf[group, :, at], x_in[group, :, at]], axis=1)
-            z_buf[group, :, at] = jnp.dot(
-                both, wz_ref[...], preferred_element_type=jnp.float32).astype(jnp.bfloat16)
-        sent = pltpu.make_async_remote_copy(
-            src_ref=z_buf.at[group], dst_ref=z_in.at[group], send_sem=ys_send.at[group],
-            recv_sem=ys_recv.at[group], device_id={"gy": 1 - gy}, device_id_type=mesh_id)
-        sent.start()
-        return sent
-
-    block = wy_ref.shape[0]
-
-    def filter_y(group, copy):
+            two[group, :, column[k]] = along_z(one, one_in, group, k).astype(jnp.bfloat16)
+        return swap(group, "gy", two, two_in, two_send, two_recv)
+
+    def y_then_send_z(group, copy):
         copy.wait_recv()
-        for b in range(plane // block):
-            at = slice(b * block, (b + 1) * block)
-            both = jnp.concatenate([z_buf[group, at, :], z_in[group, at, :]], axis=0)
-            smooth = jnp.dot(wy_ref[...], both, preferred_element_type=jnp.float32)
+        for span in spans:
+            two[group, span, :] = along_y(one, one_in, group, span).astype(jnp.bfloat16)
+        return swap(group, "gz", two, two_in, two_send, two_recv)
+
+    def end_with_z(group, copy):
+        copy.wait_recv()
+        for k in range(PAIR):
+            out_ref[group * PAIR + k] = (
+                fluid[group * PAIR + k].astype(jnp.float32) + along_z(two, two_in, group, k)
+            ).astype(jnp.bfloat16)
+
+    def end_with_y(group, copy):
+        copy.wait_recv()
+        for span in spans:
+            smooth = along_y(two, two_in, group, span)
             for k in range(PAIR):
-                out_ref[group * PAIR + k, at, :] = (
-                    fluid_ref[group * PAIR + k, at, :].astype(jnp.float32)
-                    + smooth[:, k * width_z:(k + 1) * width_z]).astype(jnp.bfloat16)
-
-    fields[0] = pay_ref[...].astype(jnp.float32)
+                out_ref[group * PAIR + k, span, :] = (
+                    fluid[group * PAIR + k, span, :].astype(jnp.float32) + smooth[:, column[k]]
+                ).astype(jnp.bfloat16)
+
     total[...] = jnp.zeros_like(total)
-    for slot in range(owners):
-        if slot:
-            sends[slot - 1].wait_recv()
-            fields[slot] = arrived[slot - 1].astype(jnp.float32)
+    for group in range(groups):
+        deposit(0, 1, group, group == 0)
+    for slot in range(1, owners):
+        sends[slot - 1].wait_recv()
+        fields[slot] = arrived[slot - 1].astype(jnp.float32)
         deposit(slot, slot + 1, 0, True)
-    z_copies, y_copies = [swap_z(0)], []
+    firsts, seconds = [begin(0, "gy")], [None]
+    for copy in loads[3:]:
+        copy.wait()
     for group in range(1, groups):
-        total[...] = jnp.zeros_like(total)
-        deposit(0, 1, group, False)
-        y_copies.append(filter_z(group - 1, z_copies[-1]))
-        deposit(1, owners, group, False)
-        z_copies.append(swap_z(group))
-    y_copies.append(filter_z(groups - 1, z_copies[-1]))
-    for group in range(groups):
-        filter_y(group, y_copies[group])
-    for copy in (*sends, *z_copies, *y_copies):
+        deposit(1, 2, group, False)
+        if group > 1:
+            seconds.append(z_then_send_y(group - 1, firsts[-1]))
+        deposit(2, owners, group, False)
+        firsts.append(begin(group, "gz"))
+    seconds.append(z_then_send_y(groups - 1, firsts[-1]))
+    seconds[0] = y_then_send_z(0, firsts[0])
+    end_with_z(0, seconds[0])
+    for group in range(1, groups):
+        end_with_y(group, seconds[group])
+    for copy in (*sends, *firsts, *seconds):
         copy.wait_send()
 
 
@@ -280,12 +337,6 @@
     channels, count_dev = parcel_values.shape
     width_x, width_y, width_z = fluid_state.shape[1:]
     owners, plane, rows = lax.axis_size("gx"), width_x * width_y, count_dev // SEG
-    is_live = jnp.arange(count_dev, dtype=jnp.int32) < live_counts[0]
-    cell_x = jnp.where(is_live, parcel_owner[:, 0] * width_x + parcel_cell // (width_y * width_z), int(FAR))
-    cell_y, cell_z = parcel_cell // width_z % width_y, parcel_cell % width_z
-    payload = jnp.concatenate(
-        [parcel_values[k].reshape(rows, SEG) for k in range(channels)]
-        + [c.astype(jnp.bfloat16).reshape(rows, SEG) for c in (cell_x, cell_y, cell_z)], axis=1)
     own_y, other_y = periodic_pair(width_y)
     repeat = np.eye(256 // width_y, dtype=np.float32)
     weight_y = np.concatenate([np.kron(repeat, own_y), np.kron(repeat, other_y)], axis=1)
@@ -293,21 +344,31 @@
     weight_z = np.concatenate([own_z.T, other_z.T], axis=0)
     sizes = (owners, channels, width_x, width_y, width_z)
     groups, wide = channels // PAIR, PAIR * width_z
-    vmem = pl.BlockSpec(memory_space=pltpu.VMEM)
+    vmem, hbm = pl.BlockSpec(memory_space=pltpu.VMEM), pl.BlockSpec(memory_space=pltpu.HBM)
+    lines = (count_dev // 128, 128)
     coupled = pl.pallas_call(
         functools.partial(fused, sizes),
         out_shape=jax.ShapeDtypeStruct((channels, plane, width_z), jnp.bfloat16),
-        in_specs=[vmem] * 4,
+        in_specs=[hbm] * 3 + [pl.BlockSpec(memory_space=pltpu.SMEM)] + [hbm] * 3,
         out_specs=vmem,
         scratch_shapes=[
+            pltpu.VMEM((channels, count_dev), jnp.bfloat16),
+            pltpu.VMEM(lines, jnp.int32),
+            pltpu.VMEM(lines, jnp.int32),
+            pltpu.VMEM((rows, (channels + FIELDS) * SEG), jnp.bfloat16),
             pltpu.VMEM((owners - 1, rows, (channels + FIELDS) * SEG), jnp.bfloat16),
             pltpu.VMEM((owners, rows, (channels + FIELDS) * SEG), jnp.float32),
+            pltpu.VMEM((channels, count_dev), jnp.float32),
             pltpu.VMEM((owners * (rows // STEP), plane, SEG * STEP), jnp.bfloat16),
-            pltpu.VMEM((plane, wide), jnp.float32),
+            pltpu.VMEM((groups, plane, wide), jnp.float32),
+            pltpu.VMEM((channels, plane, width_z), jnp.bfloat16),
+            pltpu.VMEM(weight_y.shape, jnp.bfloat16),
+            pltpu.VMEM(weight_z.shape, jnp.bfloat16),
             pltpu.VMEM((groups, plane, wide), jnp.bfloat16),
             pltpu.VMEM((groups, plane, wide), jnp.bfloat16),
             pltpu.VMEM((groups, plane, wide), jnp.bfloat16),
             pltpu.VMEM((groups, plane, wide), jnp.bfloat16),
+            pltpu.SemaphoreType.DMA((6,)),
             pltpu.SemaphoreType.DMA((owners - 1,)),
             pltpu.SemaphoreType.DMA((owners - 1,)),
             pltpu.SemaphoreType.DMA((groups,)),
@@ -316,15 +377,16 @@
             pltpu.SemaphoreType.DMA((groups,)),
         ],
         compiler_params=pltpu.CompilerParams(
-            collective_id=0, has_side_effects=True, vmem_limit_bytes=48 << 20
+            collective_id=0, has_side_effects=True, vmem_limit_bytes=63 << 20
         ),
-    )(payload, fluid_state.reshape(channels, plane, width_z),
+    )(parcel_values, parcel_owner.reshape(lines), parcel_cell.reshape(lines), live_counts,
+      fluid_state.reshape(channels, plane, width_z),
       jnp.asarray(weight_y, jnp.bfloat16), jnp.asarray(weight_z, jnp.bfloat16))
     return coupled.reshape(fluid_state.shape)
 
 
 def solution(mesh):
-    small = mesh.shape["gy"] == 2 and mesh.shape["gz"] == 2 and 2 <= mesh.shape["gx"] <= 4
+    small = mesh.shape["gy"] == 2 and mesh.shape["gz"] == 2 and 3 <= mesh.shape["gx"] <= 4
     body = on_device if small else general
     in_specs = (
         P(None, ("grp", "gx", "gy", "gz")),

time: 46.5 us -> 42.7 us (0.918)
  Pallas kernels: 41.4 us -> 39.7 us
  local copies, waits for them, and re-layouts: 3.17 us -> 2.15 us
  other arithmetic: 0.8 us -> 0 us
    pallas_call x1, Pallas kernels: 41.4 us -> 39.7 us  [on_device(): pl.pallas_call(functools.partial(fused, sizes), out_shape=jax.ShapeDtypeS...]
    mul x1 -> x0, other arithmetic: 0.77 us -> none  [on_device(): parcel_owner[:, 0] * width_x + parcel_cell // (width_y * width_z)]
    unnamed x19 -> x1, local copies, waits for them, and re-layouts: 2.82 us -> 2.15 us
where the time goes in v2:
time: 42.7 us; the launch traced here: 42.5 us
  Pallas kernels  39.7 us (93%)
  local copies, waits for them, and re-layouts  2.15 us (5%)
  between operations  0.66 us (2%)
    pallas_call x1, Pallas kernels, on_device(): pl.pallas_call(functools.partial(fused, sizes), out_shape=jax.ShapeDtypeS...  39.7 us
    unnamed x1, local copies, waits for them, and re-layouts  2.15 us

profile of v2, /device:TPU:0, one launch (start us, length us, event | category | flops | bytes accessed | tf_op | source)
XLA Modules:
  0.0 42.5 jit_solution(10138605481404022956)
XLA Ops:
  0.7 39.7 %shard_map.73 = bf16[6,512,128]{2,1,0:T(8,128)(2,1)} custom-call(bf16[6,4096]{1,0:T(8,128)(2,1)} %values_hbm.1, s32[32,128]{1,0:T(8,128)} %bitcast.6, s32[32,128]{1,0:T(8,128)} %bitcast.7, s32[1]{0:T(128)S(6)} %copy.9.live_ref, bf16[6,512,128]{2,1,0:T(8,128)(2,1)} %bitcast.5, bf16[256,512]{1,0:T(8,128)(2,1)} %constant.4.clone.wy_hbm, ...), custom_call_target="tpu_custom_call" | custom-call | tf_op jit(solution)/shard_map/pallas_call | solution.py:349
  40.4 2.1 %copy.10 = bf16[6,32,16,128]{3,2,1,0:T(8,128)(2,1)} copy(bf16[6,32,16,128]{3,2,1,0:T(8,128)(2,1)} %bitcast.4) | data formatting | bytes 1572864

commit v3 on v2

--- a/solution.py
+++ b/solution.py
@@ -225,7 +225,8 @@
 
     def field(slot, step, which):
         return jnp.concatenate(
-            [fields[slot, pl.ds(step * STEP + j, 1), which * SEG:(which + 1) * SEG] for j in range(STEP)],
+            [fields[slot, pl.ds(step * STEP + j, 1), pl.ds(pl.multiple_of(which * SEG, SEG), SEG)]
+             for j in range(STEP)],
             axis=1)
 
     def build(slot, step):
@@ -246,27 +247,29 @@
             weights[slot * steps + step], spread, (((1,), (1,)), ((), ())),
             preferred_element_type=jnp.float32)
 
-    def deposit(first, last, group, building):
-        def body(i, carry):
-            slot, step = i // steps, i % steps
-            if building:
-                build(slot, step)
+    def build_slot(slot):
+        def body(step, carry):
+            build(slot, step)
+            return carry
+
+        lax.fori_loop(0, steps, body, 0)
+
+    def add_slot(slot, group):
+        for step in range(steps):
             add(slot, step, group)
-            return carry
-
-        lax.fori_loop(first * steps, last * steps, body, 0, unroll=steps)
 
     def swap(group, axis, buffer, landing, sent, received):
         me = gy if axis == "gy" else gz
-        copy = pltpu.make_async_remote_copy(
+        return pltpu.make_async_remote_copy(
             src_ref=buffer.at[group], dst_ref=landing.at[group], send_sem=sent.at[group],
             recv_sem=received.at[group], device_id={axis: 1 - me}, device_id_type=mesh_id)
-        copy.start()
-        return copy
-
-    def begin(group, axis):
+
+    firsts = [swap(g, "gz" if g else "gy", one, one_in, one_send, one_recv) for g in range(groups)]
+    seconds = [swap(g, "gy" if g else "gz", two, two_in, two_send, two_recv) for g in range(groups)]
+
+    def begin(group):
         one[group] = total[group].astype(jnp.bfloat16)
-        return swap(group, axis, one, one_in, one_send, one_recv)
+        firsts[group].start()
 
     block = wy_hbm.shape[0]
     column = [slice(k * width_z, (k + 1) * width_z) for k in range(PAIR)]
@@ -280,17 +283,17 @@
         both = jnp.concatenate([own[group, span, :], other[group, span, :]], axis=0)
         return jnp.dot(wy[...], both, preferred_element_type=jnp.float32)
 
-    def z_then_send_y(group, copy):
-        copy.wait_recv()
+    def z_then_send_y(group):
+        firsts[group].wait_recv()
         for k in range(PAIR):
             two[group, :, column[k]] = along_z(one, one_in, group, k).astype(jnp.bfloat16)
-        return swap(group, "gy", two, two_in, two_send, two_recv)
-
-    def y_then_send_z(group, copy):
-        copy.wait_recv()
+        seconds[group].start()
+
+    def y_then_send_z(group):
+        firsts[group].wait_recv()
         for span in spans:
             two[group, span, :] = along_y(one, one_in, group, span).astype(jnp.bfloat16)
-        return swap(group, "gz", two, two_in, two_send, two_recv)
+        seconds[group].start()
 
     def end_with_z(group, copy):
         copy.wait_recv()
@@ -309,23 +312,45 @@
                 ).astype(jnp.bfloat16)
 
     total[...] = jnp.zeros_like(total)
-    for group in range(groups):
-        deposit(0, 1, group, group == 0)
-    for slot in range(1, owners):
-        sends[slot - 1].wait_recv()
-        fields[slot] = arrived[slot - 1].astype(jnp.float32)
-        deposit(slot, slot + 1, 0, True)
-    firsts, seconds = [begin(0, "gy")], [None]
+    build_slot(0)
+
+    def own(group, carry):
+        add_slot(0, group)
+        return carry
+
+    lax.fori_loop(0, groups, own, 0)
     for copy in loads[3:]:
         copy.wait()
-    for group in range(1, groups):
-        deposit(1, 2, group, False)
-        if group > 1:
-            seconds.append(z_then_send_y(group - 1, firsts[-1]))
-        deposit(2, owners, group, False)
-        firsts.append(begin(group, "gz"))
-    seconds.append(z_then_send_y(groups - 1, firsts[-1]))
-    seconds[0] = y_then_send_z(0, firsts[0])
+
+    def turn(t, carry):
+        slot, group = lax.rem(t, owners - 1) + 1, lax.div(t, owners - 1)
+
+        @pl.when(t < owners - 1)
+        def _():
+            pltpu.make_async_remote_copy(
+                src_ref=payload, dst_ref=arrived.at[slot - 1], send_sem=pay_send.at[slot - 1],
+                recv_sem=pay_recv.at[slot - 1],
+                device_id={"gx": (gx + slot) % owners}, device_id_type=mesh_id).wait_recv()
+            fields[slot] = arrived[slot - 1].astype(jnp.float32)
+            build_slot(slot)
+
+        add_slot(slot, group)
+        for g in range(groups - 1):
+            @pl.when(t == (g + 1) * (owners - 1) - 1)
+            def _(g=g):
+                begin(g)
+
+            if g:
+                @pl.when(t == (g + 1) * (owners - 1))
+                def _(g=g):
+                    z_then_send_y(g)
+
+        return carry
+
+    lax.fori_loop(0, groups * (owners - 1), turn, 0)
+    begin(groups - 1)
+    z_then_send_y(groups - 1)
+    y_then_send_z(0)
     end_with_z(0, seconds[0])
     for group in range(1, groups):
         end_with_y(group, seconds[group])

time: 42.7 us -> 40 us (0.937)
  Pallas kernels: 39.7 us -> 37.1 us
    pallas_call x1, Pallas kernels: 39.7 us -> 37.1 us  [on_device(): pl.pallas_call(functools.partial(fused, sizes), out_shape=jax.ShapeDtypeS...]
where the time goes in v3:
time: 40 us; the launch traced here: 39.9 us
  Pallas kernels  37.1 us (93%)
  local copies, waits for them, and re-layouts  2.15 us (5%)
  between operations  0.66 us (2%)
    pallas_call x1, Pallas kernels, on_device(): pl.pallas_call(functools.partial(fused, sizes), out_shape=jax.ShapeDtypeS...  37.1 us
    unnamed x1, local copies, waits for them, and re-layouts  2.15 us

profile of v3, /device:TPU:0, one launch (start us, length us, event | category | flops | bytes accessed | tf_op | source)
XLA Modules:
  0.0 39.9 jit_solution(1435237121961941505)
XLA Ops:
  0.7 37.1 %shard_map.73 = bf16[6,512,128]{2,1,0:T(8,128)(2,1)} custom-call(bf16[6,4096]{1,0:T(8,128)(2,1)} %values_hbm.1, s32[32,128]{1,0:T(8,128)} %bitcast.6, s32[32,128]{1,0:T(8,128)} %bitcast.7, s32[1]{0:T(128)S(6)} %copy.9.live_ref, bf16[6,512,128]{2,1,0:T(8,128)(2,1)} %bitcast.5, bf16[256,512]{1,0:T(8,128)(2,1)} %constant.4.clone.wy_hbm, ...), custom_call_target="tpu_custom_call" | custom-call | tf_op jit(solution)/shard_map/pallas_call | solution.py:374
  37.7 2.1 %copy.10 = bf16[6,32,16,128]{3,2,1,0:T(8,128)(2,1)} copy(bf16[6,32,16,128]{3,2,1,0:T(8,128)(2,1)} %bitcast.4) | data formatting | bytes 1572864
